TPU v7x, 32 devices: a whole 2x2x4 slice. The times are simulated.
32 devices in a mesh: dp: 8 (over z, y), seq: 4 (over x, core).
Axes of the slice: x: 2, y: 2, z: 4, core: 2. Of those that a mesh axis runs over, the one named last changes fastest.
Arguments:
- query_rows: bfloat16 [4096, 3072], P(('dp', 'seq')), may hold values from -2000 to 2000
- key_rows: bfloat16 [4096, 3072], P(('dp', 'seq')), may hold values from -2000 to 2000
- value_rows: bfloat16 [4096, 3072], P(('dp', 'seq')), may hold values from -6 to 6
- output_grad: bfloat16 [4096, 3072], P(('dp', 'seq')), may hold values from -6 to 6
- query_gain: float32 [128], replicated, may hold values from 0.5 to 5
- key_gain: float32 [128], replicated, may hold values from 0.5 to 5
- dest_groups: int32 [32, 8], P(('dp', 'seq')), may hold values from 0 to 7, each once within a row
- slot_sources: int32 [8, 32], P('dp'), may hold values from 0 to 31, each once within a row
- clip_index: int32 [8, 512], P('dp'), may hold values from 0 to 1, never falling along the last dimension, each value on 1 to 384 neighbouring positions
Outputs:
- attended: bfloat16 [4096, 3072], P(('dp', 'seq'))
- query_grad: bfloat16 [4096, 3072], P(('dp', 'seq'))
- key_grad: bfloat16 [4096, 3072], P(('dp', 'seq'))
- value_grad: bfloat16 [4096, 3072], P(('dp', 'seq'))
- gain_grads: float32 [2, 128], replicated
Inputs may be any that keep to these rules, and one draw needn't show every extreme that they name: `dest_groups`: each row names every group once. `slot_sources`: each row names every device once. `clip_index`: clip numbers never fall along a group's sequence; in each group one clip covers 128 to 384 positions and the other the rest.
All inputs are finite; a program needn't handle non-finite values.
Results may differ from a plain program's by a relative error of at most 0.003.
The roundings to bfloat16 on the way count: a program that leaves them out, or rounds other values in their place, can miss the bound.
Values may be sent and summed in bfloat16 or wider, within the bound.
A program may use at most 128 MiB of HBM per device.

v0:
```python
import jax
import jax.numpy as jnp
from jax import lax
from jax.sharding import PartitionSpec as P

EPS = 1e-06


def norm_forward(tensor, gain_vec):
    inverse = lax.rsqrt(jnp.mean(tensor * tensor, axis=-1, keepdims=True) + EPS)
    return (inverse, (tensor * inverse * gain_vec).astype(jnp.bfloat16))


def norm_backward(tensor, inverse, gain_vec, upstream):
    inner_mean = jnp.mean(gain_vec * upstream * tensor, axis=-1, keepdims=True)
    grad_input = inverse * gain_vec * upstream - tensor * inverse**3 * inner_mean
    grad_gain = jnp.sum(upstream * tensor * inverse, axis=(0, 1))
    return (grad_input.astype(jnp.bfloat16), grad_gain)


def shards(
    query_rows,
    key_rows,
    value_rows,
    output_grad,
    query_gain,
    key_gain,
    dest_groups,
    slot_sources,
    clip_index,
):
    group_count = lax.axis_size("dp")
    head_ways = lax.axis_size("seq")
    tok_rows, full_width = query_rows.shape
    head_size = query_gain.shape[0]
    heads_total = full_width // head_size
    heads_here = heads_total // head_ways
    span_width = heads_here * head_size
    block_rows = tok_rows // group_count
    source_count = group_count * head_ways
    seq_rows = tok_rows * head_ways
    targets = dest_groups[0]
    group_ids = jnp.arange(group_count, dtype=jnp.int32)
    block_order = jnp.sum(
        jnp.where(targets[None, :] == group_ids[:, None], group_ids[None, :], 0), axis=1
    )

    def pack_out(tensor):
        blocks = tensor.reshape(group_count, block_rows, head_ways, span_width)
        return jnp.take(blocks, block_order, axis=0).transpose(0, 2, 1, 3)

    send_query = pack_out(query_rows)
    send_key = pack_out(key_rows)
    send_value = pack_out(value_rows)
    send_grad = pack_out(output_grad)
    moved = (
        lax.all_to_all(
            lax.all_to_all(send_query, "dp", split_axis=0, concat_axis=0, tiled=True),
            "seq",
            split_axis=1,
            concat_axis=1,
            tiled=True,
        ),
        lax.all_to_all(
            lax.all_to_all(send_key, "dp", split_axis=0, concat_axis=0, tiled=True),
            "seq",
            split_axis=1,
            concat_axis=1,
            tiled=True,
        ),
        lax.all_to_all(
            lax.all_to_all(send_value, "dp", split_axis=0, concat_axis=0, tiled=True),
            "seq",
            split_axis=1,
            concat_axis=1,
            tiled=True,
        ),
        lax.all_to_all(
            lax.all_to_all(send_grad, "dp", split_axis=0, concat_axis=0, tiled=True),
            "seq",
            split_axis=1,
            concat_axis=1,
            tiled=True,
        ),
    )
    slot_list = slot_sources[0]

    def unpack_in(tensor):
        ordered = jnp.take(tensor.reshape(source_count, block_rows, span_width), slot_list, axis=0)
        return ordered.reshape(seq_rows, heads_here, head_size)

    query_in = unpack_in(moved[0])
    key_in = unpack_in(moved[1])
    value_in = unpack_in(moved[2])
    grad_in = unpack_in(moved[3])
    clip_row = clip_index[0]
    query_wide = query_in.astype(jnp.float32)
    key_wide = key_in.astype(jnp.float32)
    query_inv, query_norm = norm_forward(query_wide, query_gain)
    key_inv, key_norm = norm_forward(key_wide, key_gain)
    score_scale = head_size ** (-0.5)
    block_len = min(512, seq_rows)
    block_total = seq_rows // block_len

    def visit(carry, block_id):
        key_acc, value_acc = carry
        start = block_id * block_len
        query_block = lax.dynamic_slice_in_dim(query_norm, start, block_len, 0)
        grad_block = lax.dynamic_slice_in_dim(grad_in, start, block_len, 0)
        clip_block = lax.dynamic_slice_in_dim(clip_row, start, block_len, 0)
        scores = (
            jnp.einsum("qhd,khd->hqk", query_block, key_norm, preferred_element_type=jnp.float32)
            * score_scale
        )
        same_clip = (clip_block[:, None] == clip_row[None, :])[None]
        masked = jnp.where(same_clip, scores, -1e30)
        row_top = jnp.max(masked, axis=-1, keepdims=True)
        weights = jnp.exp(masked - row_top)
        probs_full = weights / jnp.sum(weights, axis=-1, keepdims=True)
        probs_low = probs_full.astype(jnp.bfloat16)
        attended = jnp.einsum(
            "hqk,khd->qhd", probs_low, value_in, preferred_element_type=jnp.float32
        )
        value_acc = value_acc + jnp.einsum(
            "hqk,qhd->khd", probs_low, grad_block, preferred_element_type=jnp.float32
        )
        prob_grad = jnp.einsum(
            "qhd,khd->hqk", grad_block, value_in, preferred_element_type=jnp.float32
        )
        row_delta = jnp.sum(grad_block.astype(jnp.float32) * attended, axis=-1).T[:, :, None]
        score_grad = (probs_full * (prob_grad - row_delta) * score_scale).astype(jnp.bfloat16)
        query_grad_block = jnp.einsum(
            "hqk,khd->qhd", score_grad, key_norm, preferred_element_type=jnp.float32
        )
        key_acc = key_acc + jnp.einsum(
            "hqk,qhd->khd", score_grad, query_block, preferred_element_type=jnp.float32
        )
        return ((key_acc, value_acc), (attended.astype(jnp.bfloat16), query_grad_block))

    zero_state = jnp.zeros((seq_rows, heads_here, head_size), jnp.float32)
    (key_grad_norm, value_grad_wide), (attended_all, query_grad_norm) = lax.scan(
        visit, (zero_state, zero_state), jnp.arange(block_total)
    )
    query_grad_norm = query_grad_norm.reshape(seq_rows, heads_here, head_size)
    attended_all = attended_all.reshape(seq_rows, heads_here, head_size)
    query_grad, query_gain_grad = norm_backward(query_wide, query_inv, query_gain, query_grad_norm)
    key_grad, key_gain_grad = norm_backward(key_wide, key_inv, key_gain, key_grad_norm)
    value_grad = value_grad_wide.astype(jnp.bfloat16)
    source_ids = jnp.arange(source_count, dtype=jnp.int32)
    slot_of = jnp.sum(
        jnp.where(slot_list[None, :] == source_ids[:, None], source_ids[None, :], 0), axis=1
    )

    def pack_back(tensor):
        ordered = jnp.take(tensor.reshape(source_count, block_rows, span_width), slot_of, axis=0)
        return ordered.reshape(group_count, head_ways, block_rows, span_width)

    back_attended = pack_back(attended_all)
    back_query = pack_back(query_grad)
    back_key = pack_back(key_grad)
    back_value = pack_back(value_grad)
    homed = (
        lax.all_to_all(
            lax.all_to_all(back_attended, "dp", split_axis=0, concat_axis=0, tiled=True),
            "seq",
            split_axis=1,
            concat_axis=1,
            tiled=True,
        ),
        lax.all_to_all(
            lax.all_to_all(back_query, "dp", split_axis=0, concat_axis=0, tiled=True),
            "seq",
            split_axis=1,
            concat_axis=1,
            tiled=True,
        ),
        lax.all_to_all(
            lax.all_to_all(back_key, "dp", split_axis=0, concat_axis=0, tiled=True),
            "seq",
            split_axis=1,
            concat_axis=1,
            tiled=True,
        ),
        lax.all_to_all(
            lax.all_to_all(back_value, "dp", split_axis=0, concat_axis=0, tiled=True),
            "seq",
            split_axis=1,
            concat_axis=1,
            tiled=True,
        ),
    )

    def home_rows(tensor):
        return jnp.take(tensor, targets, axis=0).transpose(0, 2, 1, 3).reshape(tok_rows, full_width)

    gain_query, gain_key = lax.psum((query_gain_grad, key_gain_grad), ("dp", "seq"))
    factor = float(tok_rows * source_count * heads_total) ** (-0.5)
    gain_grads = jnp.stack([gain_query, gain_key]) * factor
    return (
        home_rows(homed[0]),
        home_rows(homed[1]),
        home_rows(homed[2]),
        home_rows(homed[3]),
        gain_grads,
    )


def solution(mesh):
    return jax.shard_map(
        shards,
        mesh=mesh,
        in_specs=(
            P(("dp", "seq"), None),
            P(("dp", "seq"), None),
            P(("dp", "seq"), None),
            P(("dp", "seq"), None),
            P(),
            P(),
            P(("dp", "seq"), None),
            P("dp", None),
            P("dp", None),
        ),
        out_specs=(
            P(("dp", "seq"), None),
            P(("dp", "seq"), None),
            P(("dp", "seq"), None),
            P(("dp", "seq"), None),
            P(),
        ),
        check_vma=False,
    )
```

profile of v0, /device:TPU:0, one launch (start us, length us, event | category | flops | bytes accessed | tf_op | source)
XLA Modules:
  0.0 444.7 jit_solution(13841965842271568572)
XLA Ops:
  12.7 27.2 %all_to_all.80 = bf16[8,4,16,768]{3,2,1,0:T(8,128)(2,1)S(1)} all-to-all(bf16[8,4,16,768]{3,2,1,0:T(8,128)(2,1)S(1)} %get-tuple-element.63), channel_id=1, replica_groups=mesh['dp'=8,'seq'=4] {'dp'}, dimensions={0} | all-to-all | bytes 1572864 | tf_op jit(solution)/shard_map/all_to_all | solution.py:79
  40.0 23.2 %all_to_all.81 = bf16[8,4,16,768]{3,2,1,0:T(8,128)(2,1)S(1)} all-to-all(bf16[8,4,16,768]{3,2,1,0:T(8,128)(2,1)S(1)} %get-tuple-element.64), channel_id=1, replica_groups=mesh['dp'=8,'seq'=4] {'dp'}, dimensions={0} | all-to-all | bytes 1572864 | tf_op jit(solution)/shard_map/all_to_all | solution.py:58
  63.1 23.0 %all_to_all.82 = bf16[8,4,16,768]{3,2,1,0:T(8,128)(2,1)S(1)} all-to-all(bf16[8,4,16,768]{3,2,1,0:T(8,128)(2,1)S(1)} %get-tuple-element.65), channel_id=1, replica_groups=mesh['dp'=8,'seq'=4] {'dp'}, dimensions={0} | all-to-all | bytes 1572864 | tf_op jit(solution)/shard_map/all_to_all | solution.py:65
  86.2 3.6 all-to-all-start
  90.7 18.8 %all-to-all-done = bf16[8,4,16,768]{3,2,1,0:T(8,128)(2,1)S(1)} async-done(((bf16[8,4,16,768]{3,2,1,0:T(8,128)(2,1)}), bf16[8,4,16,768]{3,2,1,0:T(8,128)(2,1)S(1)}, u32[]{:S(2)}, u32[]{:S(2)}) %all-to-all-start) | async-done | bytes 786464 | tf_op jit(solution)/shard_map/all_to_all | solution.py:72
  109.5 3.5 all-to-all-start.9
  114.0 10.7 %all-to-all-done.9 = bf16[8,4,16,768]{3,2,0,1:T(8,128)(2,1)S(1)} async-done(((bf16[8,4,16,768]{3,2,0,1:T(8,128)(2,1)}), bf16[8,4,16,768]{3,2,0,1:T(8,128)(2,1)S(1)}, u32[]{:S(2)}, u32[]{:S(2)}) %all-to-all-start.9) | async-done | bytes 786464 | tf_op jit(solution)/shard_map/all_to_all | solution.py:78
  124.6 3.5 all-to-all-start.3
  129.1 10.7 %all-to-all-done.3 = bf16[8,4,16,768]{3,2,0,1:T(8,128)(2,1)S(1)} async-done(((bf16[8,4,16,768]{3,2,0,1:T(8,128)(2,1)}), bf16[8,4,16,768]{3,2,0,1:T(8,128)(2,1)S(1)}, u32[]{:S(2)}, u32[]{:S(2)}) %all-to-all-start.3) | async-done | bytes 786464 | tf_op jit(solution)/shard_map/all_to_all | solution.py:57
  139.8 3.5 all-to-all-start.5
  144.4 10.5 %all-to-all-done.5 = bf16[8,4,16,768]{3,2,0,1:T(8,128)(2,1)S(1)} async-done(((bf16[8,4,16,768]{3,2,0,1:T(8,128)(2,1)}), bf16[8,4,16,768]{3,2,0,1:T(8,128)(2,1)S(1)}, u32[]{:S(2)}, u32[]{:S(2)}) %all-to-all-start.5) | async-done | bytes 786464 | tf_op jit(solution)/shard_map/all_to_all | solution.py:64
  154.9 3.5 all-to-all-start.1
  166.0 4.0 all-to-all-done.1
  171.6 3.4 broadcast_select_fusion.4
  178.3 2.9 multiply_reduce_fusion
  197.6 6.5 %fusion.27 = (f32[6,512]{1,0:T(8,128)S(1)}, f32[6,512,512]{1,2,0:T(8,128)}) fusion(pred[512,512]{0,1:T(8,128)(4,1)} %broadcast_compare_fusion, bf16[512,6,128]{0,2,1:T(8,128)(2,1)} %get-tuple-element.74, bf16[512,6,128]{0,2,1:T(8,128)(2,1)} %get-tuple-element.73), kind=kOutput, calls=%fused_computation.99 | convolution fusion | flops 408945152 | bytes 8138752 | tf_op jit(solution)/shard_map/while/body/eval_jaxpr/sub | solution.py:118
  204.1 3.9 fusion.5
  219.5 2.8 reshape.187
  222.2 2.7 fusion.13
  244.1 23.2 %all_to_all.83 = bf16[8,4,16,768]{3,2,1,0:T(8,128)(2,1)S(1)} all-to-all(bf16[8,4,16,768]{3,2,1,0:T(8,128)(2,1)S(1)} %bitcast.104), channel_id=1, replica_groups=mesh['dp'=8,'seq'=4] {'dp'}, dimensions={0} | all-to-all | bytes 1572864 | tf_op jit(solution)/shard_map/all_to_all | solution.py:185
  267.4 23.2 %all_to_all.84 = bf16[8,4,16,768]{3,2,1,0:T(8,128)(2,1)S(1)} all-to-all(bf16[8,4,16,768]{3,2,1,0:T(8,128)(2,1)S(1)} %bitcast.103), channel_id=1, replica_groups=mesh['dp'=8,'seq'=4] {'dp'}, dimensions={0} | all-to-all | bytes 1572864 | tf_op jit(solution)/shard_map/all_to_all | solution.py:171
  290.5 23.0 %all_to_all.85 = bf16[8,4,16,768]{3,2,1,0:T(8,128)(2,1)S(1)} all-to-all(bf16[8,4,16,768]{3,2,1,0:T(8,128)(2,1)S(1)} %bitcast.102), channel_id=1, replica_groups=mesh['dp'=8,'seq'=4] {'dp'}, dimensions={0} | all-to-all | bytes 1572864 | tf_op jit(solution)/shard_map/all_to_all | solution.py:178
  313.6 3.6 all-to-all-start.6
  318.1 18.8 %all-to-all-done.6 = bf16[8,4,16,768]{3,2,1,0:T(8,128)(2,1)S(1)} async-done(((bf16[8,4,16,768]{3,2,1,0:T(8,128)(2,1)}), bf16[8,4,16,768]{3,2,1,0:T(8,128)(2,1)S(1)}, u32[]{:S(2)}, u32[]{:S(2)}) %all-to-all-start.6) | async-done | bytes 786464 | tf_op jit(solution)/shard_map/all_to_all | solution.py:164
  336.9 3.5 all-to-all-start.15
  341.4 10.7 %all-to-all-done.15 = bf16[8,4,16,768]{3,2,0,1:T(8,128)(2,1)S(1)} async-done(((bf16[8,4,16,768]{3,2,0,1:T(8,128)(2,1)}), bf16[8,4,16,768]{3,2,0,1:T(8,128)(2,1)S(1)}, u32[]{:S(2)}, u32[]{:S(2)}) %all-to-all-start.15) | async-done | bytes 786464 | tf_op jit(solution)/shard_map/all_to_all | solution.py:184
  352.0 3.5 all-to-all-start.11
  356.5 10.7 %all-to-all-done.11 = bf16[8,4,16,768]{3,2,0,1:T(8,128)(2,1)S(1)} async-done(((bf16[8,4,16,768]{3,2,0,1:T(8,128)(2,1)}), bf16[8,4,16,768]{3,2,0,1:T(8,128)(2,1)S(1)}, u32[]{:S(2)}, u32[]{:S(2)}) %all-to-all-start.11) | async-done | bytes 786464 | tf_op jit(solution)/shard_map/all_to_all | solution.py:170
  367.2 3.5 all-to-all-start.13
  371.6 10.7 %all-to-all-done.13 = bf16[8,4,16,768]{3,2,0,1:T(8,128)(2,1)S(1)} async-done(((bf16[8,4,16,768]{3,2,0,1:T(8,128)(2,1)}), bf16[8,4,16,768]{3,2,0,1:T(8,128)(2,1)S(1)}, u32[]{:S(2)}, u32[]{:S(2)}) %all-to-all-start.13) | async-done | bytes 786464 | tf_op jit(solution)/shard_map/all_to_all | solution.py:177
  382.3 4.2 all-to-all-start.7
  386.5 43.8 %all-reduce = (f32[1,128]{1,0:T(1,128)S(1)}, f32[1,128]{1,0:T(1,128)S(1)}) all-reduce(f32[1,128]{1,0:T(1,128)S(1)} %bitcast.121, f32[1,128]{1,0:T(1,128)S(1)} %bitcast.120), channel_id=1, replica_groups=mesh['dp'=8,'seq'=4] {'dp','seq'}, use_global_device_ids=true, to_apply=%region_12.16 | all-reduce | flops 256 | bytes 2048 | tf_op jit(solution)/shard_map/psum | solution.py:196
  (131 shorter events, 93.3 us)
Async XLA Ops:
  1.4 2.2 copy-start.8
  4.3 1.2 copy-start.9
  86.2 23.3 %all-to-all-start = ((bf16[8,4,16,768]{3,2,1,0:T(8,128)(2,1)}), bf16[8,4,16,768]{3,2,1,0:T(8,128)(2,1)S(1)}, u32[]{:S(2)}, u32[]{:S(2)}) async-start(bf16[8,4,16,768]{3,2,1,0:T(8,128)(2,1)} %get-tuple-element.66), calls=%async_computation | async-start | bytes 1572864 | tf_op jit(solution)/shard_map/all_to_all | solution.py:72
  109.5 15.1 %all-to-all-start.9 = ((bf16[8,4,16,768]{3,2,0,1:T(8,128)(2,1)}), bf16[8,4,16,768]{3,2,0,1:T(8,128)(2,1)S(1)}, u32[]{:S(2)}, u32[]{:S(2)}) async-start(bf16[8,4,16,768]{3,2,0,1:T(8,128)(2,1)} %copy.291), calls=%async_computation.9 | async-start | bytes 1572864 | tf_op jit(solution)/shard_map/all_to_all | solution.py:78
  124.6 15.1 %all-to-all-start.3 = ((bf16[8,4,16,768]{3,2,0,1:T(8,128)(2,1)}), bf16[8,4,16,768]{3,2,0,1:T(8,128)(2,1)S(1)}, u32[]{:S(2)}, u32[]{:S(2)}) async-start(bf16[8,4,16,768]{3,2,0,1:T(8,128)(2,1)} %copy.273), calls=%async_computation.3 | async-start | bytes 1572864 | tf_op jit(solution)/shard_map/all_to_all | solution.py:57
  128.1 15.1 %copy-start.13 = (s32[1,32]{1,0:T(1,128)S(1)}, s32[1,32]{1,0:T(1,128)}, u32[]{:S(2)}) copy-start(s32[1,32]{1,0:T(1,128)} %param.22) | copy-start | bytes 388
  139.8 15.1 %all-to-all-start.5 = ((bf16[8,4,16,768]{3,2,0,1:T(8,128)(2,1)}), bf16[8,4,16,768]{3,2,0,1:T(8,128)(2,1)S(1)}, u32[]{:S(2)}, u32[]{:S(2)}) async-start(bf16[8,4,16,768]{3,2,0,1:T(8,128)(2,1)} %copy.278), calls=%async_computation.5 | async-start | bytes 1572864 | tf_op jit(solution)/shard_map/all_to_all | solution.py:64
  143.4 15.0 %copy-start.10 = (s32[1,512]{1,0:T(1,128)S(1)}, s32[1,512]{1,0:T(1,128)}, u32[]{:S(2)}) copy-start(s32[1,512]{1,0:T(1,128)} %param.23) | copy-start | bytes 6148
  154.9 15.1 %all-to-all-start.1 = ((bf16[8,4,16,768]{3,2,0,1:T(8,128)(2,1)}), bf16[8,4,16,768]{3,2,0,1:T(8,128)(2,1)S(1)}, u32[]{:S(2)}, u32[]{:S(2)}) async-start(bf16[8,4,16,768]{3,2,0,1:T(8,128)(2,1)} %copy.270), calls=%async_computation.1 | async-start | bytes 1572864 | tf_op jit(solution)/shard_map/all_to_all | solution.py:71
  191.9 4.0 copy-start.11
  191.9 4.0 copy-start.12
  204.1 3.9 copy-start
  204.1 7.5 %slice-start = ((s8[6291456]{0:T(1024)(128)(4,1)}), s8[4194304]{0:T(1024)(128)(4,1)S(1)}, s32[]{:S(2)}) async-start(s8[6291456]{0:T(1024)(128)(4,1)} %bitcast.100), calls=%async_computation.16 | async-start | bytes 8388608
  208.0 2.0 copy-start.2
  208.0 3.6 slice-start.1
  211.6 1.2 copy-start.7
  212.8 1.9 copy-start.6
  228.4 5.3 %copy-start.1 = (f32[6,128,512]{2,1,0:T(8,128)S(1)}, f32[6,128,512]{2,1,0:T(8,128)}, u32[]{:S(2)}) copy-start(f32[6,128,512]{2,1,0:T(8,128)} %get-tuple-element.72) | copy-start | bytes 4718596
  237.0 1.5 copy-start.5
  239.3 3.5 copy-start.3
  239.3 3.5 copy-start.4
  313.6 23.3 %all-to-all-start.6 = ((bf16[8,4,16,768]{3,2,1,0:T(8,128)(2,1)}), bf16[8,4,16,768]{3,2,1,0:T(8,128)(2,1)S(1)}, u32[]{:S(2)}, u32[]{:S(2)}) async-start(bf16[8,4,16,768]{3,2,1,0:T(8,128)(2,1)} %bitcast.10), calls=%async_computation.6 | async-start | bytes 1572864 | tf_op jit(solution)/shard_map/all_to_all | solution.py:164
  336.9 15.1 %all-to-all-start.15 = ((bf16[8,4,16,768]{3,2,0,1:T(8,128)(2,1)}), bf16[8,4,16,768]{3,2,0,1:T(8,128)(2,1)S(1)}, u32[]{:S(2)}, u32[]{:S(2)}) async-start(bf16[8,4,16,768]{3,2,0,1:T(8,128)(2,1)} %copy.314), calls=%async_computation.15 | async-start | bytes 1572864 | tf_op jit(solution)/shard_map/all_to_all | solution.py:184
  352.0 15.1 %all-to-all-start.11 = ((bf16[8,4,16,768]{3,2,0,1:T(8,128)(2,1)}), bf16[8,4,16,768]{3,2,0,1:T(8,128)(2,1)S(1)}, u32[]{:S(2)}, u32[]{:S(2)}) async-start(bf16[8,4,16,768]{3,2,0,1:T(8,128)(2,1)} %copy.301), calls=%async_computation.11 | async-start | bytes 1572864 | tf_op jit(solution)/shard_map/all_to_all | solution.py:170
  367.2 15.1 %all-to-all-start.13 = ((bf16[8,4,16,768]{3,2,0,1:T(8,128)(2,1)}), bf16[8,4,16,768]{3,2,0,1:T(8,128)(2,1)S(1)}, u32[]{:S(2)}, u32[]{:S(2)}) async-start(bf16[8,4,16,768]{3,2,0,1:T(8,128)(2,1)} %copy.308), calls=%async_computation.13 | async-start | bytes 1572864 | tf_op jit(solution)/shard_map/all_to_all | solution.py:177
  370.7 15.8 %copy-start.14 = (s32[1,8]{1,0:T(1,128)S(1)}, s32[1,8]{1,0:T(1,128)}, u32[]{:S(2)}) copy-start(s32[1,8]{1,0:T(1,128)} %param.21) | copy-start | bytes 100
  382.3 52.6 %all-to-all-start.7 = ((bf16[8,4,16,768]{3,2,0,1:T(8,128)(2,1)}), bf16[8,4,16,768]{3,2,0,1:T(8,128)(2,1)}, u32[]{:S(2)}, u32[]{:S(2)}) async-start(bf16[8,4,16,768]{3,2,0,1:T(8,128)(2,1)} %copy.287), calls=%async_computation.7 | async-start | bytes 1572864 | tf_op jit(solution)/shard_map/all_to_all | solution.py:163
where the time goes:
time: 446 us; the launch traced here: 445 us
  blocking collectives  187 us (42%)
  waiting for transfers between devices  105 us (24%)
  local copies, waits for them, and re-layouts  76.5 us (17%)
  starting transfers between devices  35.8 us (8%)
  other arithmetic  23.4 us (5%)
  matrix products  15.5 us (3%)
    psum x1, blocking collectives, shards(): lax.psum((query_gain_grad, key_gain_grad), ('dp', 'seq'))  43.8 us
    all_to_all x1, blocking collectives, shards(): lax.all_to_all(send_grad, 'dp', split_axis=0, concat_axis=0, tiled=True)  27.2 us
    all_to_all x1, blocking collectives, shards(): lax.all_to_all(back_value, 'dp', split_axis=0, concat_axis=0, tiled=True)  23.2 us
    all_to_all x1, blocking collectives, shards(): lax.all_to_all(send_query, 'dp', split_axis=0, concat_axis=0, tiled=True)  23.2 us
    all_to_all x1, blocking collectives, shards(): lax.all_to_all(back_query, 'dp', split_axis=0, concat_axis=0, tiled=True)  23.2 us
    all_to_all x1, blocking collectives, shards(): lax.all_to_all(send_key, 'dp', split_axis=0, concat_axis=0, tiled=True)  23 us
    all_to_all x1, blocking collectives, shards(): lax.all_to_all(back_key, 'dp', split_axis=0, concat_axis=0, tiled=True)  23 us
    all_to_all x1, waiting for transfers between devices, shards(): lax.all_to_all(send_value, 'dp', split_axis=0, concat_axis=0, tiled=True)  18.8 us
  transfers between devices with their start and end apart: 10, of which 9 were waited for; matrix products, arithmetic and copies ran while one was open for 4% of the time, Pallas kernels for 0%

commit v1 on v0

--- a/solution.py
+++ b/solution.py
@@ -1,6 +1,10 @@
+import functools
+
 import jax
 import jax.numpy as jnp
 from jax import lax
+from jax.experimental import pallas as pl
+from jax.experimental.pallas import tpu as pltpu
 from jax.sharding import PartitionSpec as P
 
 EPS = 1e-06
@@ -18,7 +22,7 @@
     return (grad_input.astype(jnp.bfloat16), grad_gain)
 
 
-def shards(
+def shards_plain(
     query_rows,
     key_rows,
     value_rows,
@@ -205,6 +209,298 @@
     )
 
 
+MESH = pl.DeviceIdType.MESH
+NT = (((1,), (1,)), ((), ()))
+TN = (((0,), (0,)), ((), ()))
+NN = (((1,), (0,)), ((), ()))
+
+
+def dot(a, b, dims):
+    return lax.dot_general(a, b, dims, preferred_element_type=jnp.float32)
+
+
+def fused_kernel(
+    dims,
+    dest_ref,
+    slot_ref,
+    clip_ref,
+    qgain_ref,
+    kgain_ref,
+    q_ref,
+    k_ref,
+    v_ref,
+    do_ref,
+    att_ref,
+    qg_ref,
+    kg_ref,
+    vg_ref,
+    gain_ref,
+    stage,
+    recv,
+    back,
+    bias,
+    gstage,
+    grecv,
+    order,
+    send_sem,
+    recv_sem,
+    back_send_sem,
+    back_recv_sem,
+    gain_send_sem,
+    gain_recv_sem,
+    *homes,
+):
+    groups, ways, rows, chunks, width, heads, factor = dims
+    n = groups * ways
+    seq = n * rows
+    span = chunks * width
+    ins = (q_ref, k_ref, v_ref, do_ref)
+    outs = (att_ref, qg_ref, kg_ref, vg_ref)
+    me = lax.axis_index("dp") * ways + lax.axis_index("seq")
+    stride = n // 2 + 1
+
+    def peer(i):
+        other = (me + i * stride) % n
+        return other, (other // ways, other % ways)
+
+    barrier = pltpu.get_barrier_semaphore()
+
+    @pl.loop(1, n)
+    def _(i):
+        pl.semaphore_signal(barrier, inc=1, device_id=peer(i)[1], device_id_type=MESH)
+
+    def pack(c):
+        for t in range(4):
+            for s in range(ways):
+                part = ins[t][:, s * span + c * width : s * span + (c + 1) * width]
+                part = dot(order[...], part, NN).astype(jnp.bfloat16)
+                for g in range(groups):
+                    stage[c, g * ways + s, t * rows : (t + 1) * rows, :] = part[
+                        g * rows : (g + 1) * rows
+                    ]
+
+    def send_all(c):
+        @pl.loop(1, n)
+        def _(i):
+            other, where = peer(i)
+            pltpu.make_async_remote_copy(
+                src_ref=stage.at[c, other],
+                dst_ref=recv.at[c, me],
+                send_sem=send_sem.at[c],
+                recv_sem=recv_sem.at[c],
+                device_id=where,
+                device_id_type=MESH,
+            ).start()
+
+        recv[c, me] = stage[c, me]
+
+    def return_all(c):
+        @pl.loop(1, n)
+        def _(i):
+            other, where = peer(i)
+            pltpu.make_async_remote_copy(
+                src_ref=back.at[c, other],
+                dst_ref=homes[c].at[me],
+                send_sem=back_send_sem.at[c],
+                recv_sem=back_recv_sem.at[c],
+                device_id=where,
+                device_id_type=MESH,
+            ).start()
+
+        homes[c][me] = back[c, me]
+
+    def wait_bytes(ref, sem):
+        pltpu.make_async_copy(ref, ref, sem).wait()
+
+    row = lax.broadcasted_iota(jnp.int32, order.shape, 0)
+    col = lax.broadcasted_iota(jnp.int32, order.shape, 1)
+    joins = jnp.zeros(order.shape, jnp.int32)
+    for j in range(groups):
+        joins = joins + jnp.where(col // rows == j, dest_ref[0, j], 0)
+    same = (row // rows == joins) & (row % rows == col % rows)
+    order[...] = jnp.where(same, 1.0, 0.0).astype(jnp.bfloat16)
+
+    pack(0)
+    pl.semaphore_wait(barrier, n - 1)
+    send_all(0)
+    for c in range(1, chunks):
+        pack(c)
+        send_all(c)
+
+    zeros = jnp.sum(jnp.where(clip_ref[...] == 0, 1.0, 0.0), axis=1, keepdims=True)
+    lane = lax.broadcasted_iota(jnp.int32, (8, seq), 1)
+    sub = lax.broadcasted_iota(jnp.int32, (seq, 128), 0)
+    lane_src, sub_src = lane // rows, sub // rows
+    lane_pos, sub_pos = lane % rows, sub % rows
+    for t in range(n):
+        src = slot_ref[0, t]
+        lane_pos = lane_pos + jnp.where(lane_src == src, t * rows, 0)
+        sub_pos = sub_pos + jnp.where(sub_src == src, t * rows, 0)
+    lane_clip = jnp.where(lane_pos.astype(jnp.float32) >= zeros, 1.0, 0.0)[0:1]
+    sub_clip = jnp.where(sub_pos.astype(jnp.float32) >= zeros, 1.0, 0.0)[:, 0:1]
+    bias[...] = jnp.where(lane_clip == sub_clip, 0.0, -1e30)
+    gstage[...] = jnp.zeros_like(gstage)
+
+    hd = qgain_ref.shape[1]
+    scale = hd ** (-0.5)
+    gain_q = qgain_ref[...]
+    gain_k = kgain_ref[...]
+
+    def head_of(c, h):
+        cols = pl.ds(pl.multiple_of(h * hd, hd), hd)
+
+        def take(t):
+            return recv[c, :, t * rows : (t + 1) * rows, cols].reshape(seq, hd)
+
+        gq = take(0).astype(jnp.float32)
+        gk = take(1).astype(jnp.float32)
+        gv = take(2)
+        gdo = take(3)
+        rq = lax.rsqrt(jnp.mean(gq * gq, axis=-1, keepdims=True) + EPS)
+        rk = lax.rsqrt(jnp.mean(gk * gk, axis=-1, keepdims=True) + EPS)
+        qn = (gq * rq * gain_q).astype(jnp.bfloat16)
+        kn = (gk * rk * gain_k).astype(jnp.bfloat16)
+        masked = dot(qn, kn, NT) * scale + bias[...]
+        weights = jnp.exp(masked - jnp.max(masked, axis=-1, keepdims=True))
+        probs = weights / jnp.sum(weights, axis=-1, keepdims=True)
+        low = probs.astype(jnp.bfloat16)
+        att = dot(low, gv, NN)
+        dv = dot(low, gdo, TN)
+        dp = dot(gdo, gv, NT)
+        delta = jnp.sum(gdo.astype(jnp.float32) * att, axis=-1, keepdims=True)
+        ds = (probs * (dp - delta) * scale).astype(jnp.bfloat16)
+        dqn = dot(ds, kn, NN)
+        dkn = dot(ds, qn, TN)
+        mq = jnp.mean(gain_q * dqn * gq, axis=-1, keepdims=True)
+        mk = jnp.mean(gain_k * dkn * gk, axis=-1, keepdims=True)
+        dq = rq * gain_q * dqn - gq * (rq * rq * rq) * mq
+        dk = rk * gain_k * dkn - gk * (rk * rk * rk) * mk
+        gstage[0:1, :] += jnp.sum(dqn * gq * rq, axis=0, keepdims=True)
+        gstage[1:2, :] += jnp.sum(dkn * gk * rk, axis=0, keepdims=True)
+        for t, res in enumerate((att, dq, dk, dv)):
+            back[c, :, t * rows : (t + 1) * rows, cols] = res.astype(jnp.bfloat16).reshape(
+                n, rows, hd
+            )
+
+    for c in range(chunks):
+        wait_bytes(recv.at[c, pl.ds(0, n - 1)], recv_sem.at[c])
+
+        @pl.loop(0, heads)
+        def _(h):
+            head_of(c, h)
+
+        if c == chunks - 1:
+            @pl.loop(1, n)
+            def _(i):
+                pltpu.make_async_remote_copy(
+                    src_ref=gstage,
+                    dst_ref=grecv.at[me],
+                    send_sem=gain_send_sem,
+                    recv_sem=gain_recv_sem,
+                    device_id=peer(i)[1],
+                    device_id_type=MESH,
+                ).start()
+
+            grecv[me] = gstage[...]
+        return_all(c)
+
+    for c in range(chunks):
+        wait_bytes(homes[c].at[pl.ds(0, n - 1)], back_recv_sem.at[c])
+
+        for s in range(ways):
+            for t in range(4):
+                part = jnp.concatenate(
+                    [
+                        homes[c][g * ways + s, t * rows : (t + 1) * rows, :]
+                        for g in range(groups)
+                    ],
+                    axis=0,
+                )
+                outs[t][:, s * span + c * width : s * span + (c + 1) * width] = dot(
+                    order[...], part, TN
+                ).astype(jnp.bfloat16)
+
+    wait_bytes(grecv.at[pl.ds(0, n - 1)], gain_recv_sem)
+    gain_ref[...] = jnp.sum(grecv[...], axis=0)[0:2] * factor
+    for c in range(chunks):
+        wait_bytes(stage.at[c, pl.ds(0, n - 1)], send_sem.at[c])
+        wait_bytes(back.at[c, pl.ds(0, n - 1)], back_send_sem.at[c])
+    wait_bytes(grecv.at[pl.ds(0, n - 1)], gain_send_sem)
+
+
+def shards_fused(
+    query_rows,
+    key_rows,
+    value_rows,
+    output_grad,
+    query_gain,
+    key_gain,
+    dest_groups,
+    slot_sources,
+    clip_index,
+):
+    groups = lax.axis_size("dp")
+    ways = lax.axis_size("seq")
+    n = groups * ways
+    tok, full = query_rows.shape
+    hd = query_gain.shape[0]
+    rows = tok // groups
+    heads_here = full // hd // ways
+    heads = 2 if heads_here % 2 == 0 else 1
+    chunks = heads_here // heads
+    width = heads * hd
+    seq = tok * ways
+    factor = float(tok * n * (full // hd)) ** (-0.5)
+    dims = (groups, ways, rows, chunks, width, heads, factor)
+    vmem = pl.BlockSpec(memory_space=pltpu.VMEM)
+    smem = pl.BlockSpec(memory_space=pltpu.SMEM)
+    slab = (n, 4 * rows, width)
+    bf = jnp.bfloat16
+    out = jax.ShapeDtypeStruct((tok, full), bf)
+    dma = pltpu.SemaphoreType.DMA
+    return pl.pallas_call(
+        functools.partial(fused_kernel, dims),
+        out_shape=(out, out, out, out, jax.ShapeDtypeStruct((2, hd), jnp.float32)),
+        in_specs=[smem, smem] + [vmem] * 7,
+        out_specs=(vmem,) * 5,
+        scratch_shapes=[
+            pltpu.VMEM((chunks,) + slab, bf),
+            pltpu.VMEM((chunks,) + slab, bf),
+            pltpu.VMEM((chunks,) + slab, bf),
+            pltpu.VMEM((seq, seq), jnp.float32),
+            pltpu.VMEM((8, hd), jnp.float32),
+            pltpu.VMEM((n, 8, hd), jnp.float32),
+            pltpu.VMEM((tok, tok), bf),
+            dma((chunks,)),
+            dma((chunks,)),
+            dma((chunks,)),
+            dma((chunks,)),
+            dma,
+            dma,
+        ]
+        + [pltpu.VMEM(slab, bf)] * chunks,
+        compiler_params=pltpu.CompilerParams(
+            collective_id=0, has_side_effects=True, vmem_limit_bytes=48 * 2**20
+        ),
+    )(
+        dest_groups,
+        slot_sources,
+        clip_index,
+        query_gain.reshape(1, hd),
+        key_gain.reshape(1, hd),
+        query_rows,
+        key_rows,
+        value_rows,
+        output_grad,
+    )
+
+
+def shards(query_rows, *rest):
+    if (query_rows.shape[0] // lax.axis_size("dp")) % 16 == 0:
+        return shards_fused(query_rows, *rest)
+    return shards_plain(query_rows, *rest)
+
+
 def solution(mesh):
     return jax.shard_map(
         shards,

time: 446 us -> 158 us (0.35)
  blocking collectives: 187 us -> 0 us
  Pallas kernels: 0 us -> 148 us
  waiting for transfers between devices: 105 us -> 0 us
  local copies, waits for them, and re-layouts: 76.5 us -> 8.8 us
  starting transfers between devices: 35.8 us -> 0 us
  other arithmetic: 23.4 us -> 0 us
  matrix products: 15.5 us -> 0 us
    pallas_call x0 -> x1, Pallas kernels: none -> 148 us  [shards_fused(): pl.pallas_call(functools.partial(fused_kernel, dims), out_shape=(out, out...]
    all_to_all x6 -> x0, blocking collectives: 143 us -> none  [the longest x1 27.2 us: shards(): lax.all_to_all(send_grad, 'dp', split_axis=0, concat_axis=0, tiled=True)]
    all_to_all x10 -> x0, waiting for transfers between devices: 105 us -> none  [the longest x1 18.8 us: shards(): lax.all_to_all(send_value, 'dp', split_axis=0, concat_axis=0, tiled=True)]
    psum x1 -> x0, blocking collectives: 43.8 us -> none  [shards(): lax.psum((query_gain_grad, key_gain_grad), ('dp', 'seq'))]
    all_to_all x10 -> x0, starting transfers between devices: 35.8 us -> none  [the longest x1 4.2 us: shards(): lax.all_to_all(lax.all_to_all(back_attended, 'dp', split_axis=0, concat_a...]
    gather x16 -> x0, local copies, waits for them, and re-layouts: 22.9 us -> none  [the longest x4 7.66 us: pack_back(): jnp.take(tensor.reshape(source_count, block_rows, span_width), slot_of, a...]
    reshape x14 -> x0, local copies, waits for them, and re-layouts: 19.6 us -> none  [the longest x3 7.77 us: unpack_in(): return ordered.reshape(seq_rows, heads_here, head_size)]
    convert_element_type x8 -> x0, local copies, waits for them, and re-layouts: 13.5 us -> none  [the longest x2 3.57 us: norm_backward(): return (grad_input.astype(jnp.bfloat16), grad_gain)]
  transfers between devices with their start and end apart: 10 -> 0, of which waited for: 9 -> 0; matrix products, arithmetic and copies ran while one was open for 4% -> 0% of each run, Pallas kernels for 0% -> 0%
where the time goes in v1:
time: 158 us; the launch traced here: 157 us
  Pallas kernels  148 us (94%)
  local copies, waits for them, and re-layouts  8.8 us (6%)
    pallas_call x1, Pallas kernels, shards_fused(): pl.pallas_call(functools.partial(fused_kernel, dims), out_shape=(out, out...  148 us
    unnamed x21, local copies, waits for them, and re-layouts  8.8 us

profile of v1, /device:TPU:0, one launch (start us, length us, event | category | flops | bytes accessed | tf_op | source)
XLA Modules:
  0.0 157.2 jit_solution(16890158269141024641)
XLA Ops:
  0.6 0.0 copy-start.3
  0.6 0.0 copy-start.4
  0.7 0.0 copy-start.5
  0.7 0.0 copy-start.6
  0.7 0.6 copy-done.3
  1.3 0.0 copy-done.4
  1.3 0.0 copy-done.5
  1.3 0.0 copy-done.6
  1.3 0.0 copy-start
  1.3 1.1 copy-done
  2.5 0.0 copy-start.1
  2.5 1.1 copy-done.1
  3.6 0.0 copy-start.2
  3.6 1.1 copy-done.2
  4.7 0.0 copy-start.7
  4.7 0.7 copy-done.7
  5.4 147.7 %shard_map.128 = (bf16[128,3072]{1,0:T(8,128)(2,1)S(1)}, bf16[128,3072]{1,0:T(8,128)(2,1)S(1)}, bf16[128,3072]{1,0:T(8,128)(2,1)S(1)}, bf16[128,3072]{1,0:T(8,128)(2,1)S(1)}, f32[2,128]{1,0:T(2,128)S(1)}) custom-call(s32[1,8]{1,0:T(1,128)S(1)} %copy-done.4, s32[1,32]{1,0:T(1,128)S(1)} %copy-done.5, s32[1,512]{1,0:T(1,128)S(1)} %copy-done.3, ...), custom_call_target="tpu_custom_call" | custom-call | tf_op jit(solution)/shard_map/pallas_call | solution.py:461
  153.1 0.9 copy.19
  154.0 0.9 copy.20
  154.9 0.9 copy.21
  155.8 0.9 copy.22
  156.6 0.6 copy.23
Async XLA Ops:
  0.6 0.7 copy-start.3
  0.6 0.7 copy-start.4
  0.7 0.7 copy-start.5
  0.7 0.7 copy-start.6
  1.3 1.1 copy-start
  2.5 1.1 copy-start.1
  3.6 1.1 copy-start.2
  4.7 0.7 copy-start.7

commit v2 on v1

--- a/solution.py
+++ b/solution.py
@@ -219,6 +219,48 @@
     return lax.dot_general(a, b, dims, preferred_element_type=jnp.float32)
 
 
+def block_order(dest_ref, groups, rows):
+    shape = (groups * rows, groups * rows)
+    row = lax.broadcasted_iota(jnp.int32, shape, 0)
+    col = lax.broadcasted_iota(jnp.int32, shape, 1)
+    joins = jnp.zeros(shape, jnp.int32)
+    for j in range(groups):
+        joins = joins + jnp.where(col // rows == j, dest_ref[0, j], 0)
+    same = (row // rows == joins) & (row % rows == col % rows)
+    return jnp.where(same, 1.0, 0.0).astype(jnp.bfloat16)
+
+
+def home_kernel(dims, factor, dest_ref, grecv, *refs):
+    groups, ways, rows, chunks, width, heads = dims
+    span = chunks * width
+    homes, outs = refs[:chunks], refs[chunks : chunks + 4]
+    gain_ref, held, sem, got, got_sem = refs[chunks + 4 :]
+    joins = [dest_ref[0, j] for j in range(groups)]
+    loads = [pltpu.make_async_copy(homes[c], got.at[c], got_sem.at[c]) for c in range(chunks)]
+    for load in loads:
+        load.start()
+    for load in loads:
+        load.wait()
+    copies = []
+    for t in range(4):
+        for c in range(chunks):
+            for s in range(ways):
+                for j in range(groups):
+                    held[
+                        t,
+                        j * rows : (j + 1) * rows,
+                        s * span + c * width : s * span + (c + 1) * width,
+                    ] = got[c, joins[j] * ways + s, t * rows : (t + 1) * rows, :]
+        copies.append(pltpu.make_async_copy(held.at[t], outs[t], sem.at[t]))
+        copies[t].start()
+    hd = gain_ref.shape[1]
+    total = jnp.sum(grecv[...], axis=0) * factor
+    gain_ref[0:1, :] = total[:, 0:hd]
+    gain_ref[1:2, :] = total[:, hd : 2 * hd]
+    for copy in copies:
+        copy.wait()
+
+
 def fused_kernel(
     dims,
     dest_ref,
@@ -230,32 +272,18 @@
     k_ref,
     v_ref,
     do_ref,
-    att_ref,
-    qg_ref,
-    kg_ref,
-    vg_ref,
-    gain_ref,
-    stage,
-    recv,
-    back,
-    bias,
-    gstage,
     grecv,
-    order,
-    send_sem,
-    recv_sem,
-    back_send_sem,
-    back_recv_sem,
-    gain_send_sem,
-    gain_recv_sem,
-    *homes,
+    *rest,
 ):
-    groups, ways, rows, chunks, width, heads, factor = dims
+    groups, ways, rows, chunks, width, heads = dims
+    homes = rest[:chunks]
+    stage, recv, back, bias, gstage, order, rows_in = rest[chunks : chunks + 7]
+    in_sem, send_sem, recv_sem, back_send_sem, back_recv_sem = rest[chunks + 7 : chunks + 12]
+    own_sem, gain_send_sem, gain_recv_sem = rest[chunks + 12 :]
     n = groups * ways
     seq = n * rows
     span = chunks * width
     ins = (q_ref, k_ref, v_ref, do_ref)
-    outs = (att_ref, qg_ref, kg_ref, vg_ref)
     me = lax.axis_index("dp") * ways + lax.axis_index("seq")
     stride = n // 2 + 1
 
@@ -263,6 +291,9 @@
         other = (me + i * stride) % n
         return other, (other // ways, other % ways)
 
+    loads = [pltpu.make_async_copy(ins[t], rows_in.at[t], in_sem.at[t]) for t in range(4)]
+    for load in loads:
+        load.start()
     barrier = pltpu.get_barrier_semaphore()
 
     @pl.loop(1, n)
@@ -272,7 +303,7 @@
     def pack(c):
         for t in range(4):
             for s in range(ways):
-                part = ins[t][:, s * span + c * width : s * span + (c + 1) * width]
+                part = rows_in[t, :, s * span + c * width : s * span + (c + 1) * width]
                 part = dot(order[...], part, NN).astype(jnp.bfloat16)
                 for g in range(groups):
                     stage[c, g * ways + s, t * rows : (t + 1) * rows, :] = part[
@@ -307,18 +338,14 @@
                 device_id_type=MESH,
             ).start()
 
-        homes[c][me] = back[c, me]
+        pltpu.make_async_copy(back.at[c, me], homes[c].at[me], own_sem.at[c]).start()
 
     def wait_bytes(ref, sem):
         pltpu.make_async_copy(ref, ref, sem).wait()
 
-    row = lax.broadcasted_iota(jnp.int32, order.shape, 0)
-    col = lax.broadcasted_iota(jnp.int32, order.shape, 1)
-    joins = jnp.zeros(order.shape, jnp.int32)
-    for j in range(groups):
-        joins = joins + jnp.where(col // rows == j, dest_ref[0, j], 0)
-    same = (row // rows == joins) & (row % rows == col % rows)
-    order[...] = jnp.where(same, 1.0, 0.0).astype(jnp.bfloat16)
+    order[...] = block_order(dest_ref, groups, rows)
+    for load in loads:
+        load.wait()
 
     pack(0)
     pl.semaphore_wait(barrier, n - 1)
@@ -375,8 +402,8 @@
         mk = jnp.mean(gain_k * dkn * gk, axis=-1, keepdims=True)
         dq = rq * gain_q * dqn - gq * (rq * rq * rq) * mq
         dk = rk * gain_k * dkn - gk * (rk * rk * rk) * mk
-        gstage[0:1, :] += jnp.sum(dqn * gq * rq, axis=0, keepdims=True)
-        gstage[1:2, :] += jnp.sum(dkn * gk * rk, axis=0, keepdims=True)
+        gstage[:, 0:hd] += jnp.sum(dqn * gq * rq, axis=0, keepdims=True)
+        gstage[:, hd : 2 * hd] += jnp.sum(dkn * gk * rk, axis=0, keepdims=True)
         for t, res in enumerate((att, dq, dk, dv)):
             back[c, :, t * rows : (t + 1) * rows, cols] = res.astype(jnp.bfloat16).reshape(
                 n, rows, hd
@@ -406,25 +433,11 @@
 
     for c in range(chunks):
         wait_bytes(homes[c].at[pl.ds(0, n - 1)], back_recv_sem.at[c])
-
-        for s in range(ways):
-            for t in range(4):
-                part = jnp.concatenate(
-                    [
-                        homes[c][g * ways + s, t * rows : (t + 1) * rows, :]
-                        for g in range(groups)
-                    ],
-                    axis=0,
-                )
-                outs[t][:, s * span + c * width : s * span + (c + 1) * width] = dot(
-                    order[...], part, TN
-                ).astype(jnp.bfloat16)
-
     wait_bytes(grecv.at[pl.ds(0, n - 1)], gain_recv_sem)
-    gain_ref[...] = jnp.sum(grecv[...], axis=0)[0:2] * factor
     for c in range(chunks):
         wait_bytes(stage.at[c, pl.ds(0, n - 1)], send_sem.at[c])
         wait_bytes(back.at[c, pl.ds(0, n - 1)], back_send_sem.at[c])
+        pltpu.make_async_copy(back.at[c, me], homes[c].at[me], own_sem.at[c]).wait()
     wait_bytes(grecv.at[pl.ds(0, n - 1)], gain_send_sem)
 
 
@@ -451,36 +464,39 @@
     width = heads * hd
     seq = tok * ways
     factor = float(tok * n * (full // hd)) ** (-0.5)
-    dims = (groups, ways, rows, chunks, width, heads, factor)
+    dims = (groups, ways, rows, chunks, width, heads)
     vmem = pl.BlockSpec(memory_space=pltpu.VMEM)
     smem = pl.BlockSpec(memory_space=pltpu.SMEM)
     slab = (n, 4 * rows, width)
     bf = jnp.bfloat16
     out = jax.ShapeDtypeStruct((tok, full), bf)
     dma = pltpu.SemaphoreType.DMA
-    return pl.pallas_call(
+    hbm = pl.BlockSpec(memory_space=pl.ANY)
+    landed = pl.pallas_call(
         functools.partial(fused_kernel, dims),
-        out_shape=(out, out, out, out, jax.ShapeDtypeStruct((2, hd), jnp.float32)),
-        in_specs=[smem, smem] + [vmem] * 7,
-        out_specs=(vmem,) * 5,
+        out_shape=[jax.ShapeDtypeStruct((n, 1, 2 * hd), jnp.float32)]
+        + [jax.ShapeDtypeStruct(slab, bf)] * chunks,
+        in_specs=[smem, smem] + [vmem] * 3 + [hbm] * 4,
+        out_specs=[vmem] + [hbm] * chunks,
         scratch_shapes=[
             pltpu.VMEM((chunks,) + slab, bf),
             pltpu.VMEM((chunks,) + slab, bf),
             pltpu.VMEM((chunks,) + slab, bf),
             pltpu.VMEM((seq, seq), jnp.float32),
-            pltpu.VMEM((8, hd), jnp.float32),
-            pltpu.VMEM((n, 8, hd), jnp.float32),
+            pltpu.VMEM((1, 2 * hd), jnp.float32),
             pltpu.VMEM((tok, tok), bf),
+            pltpu.VMEM((4, tok, full), bf),
+            dma((4,)),
+            dma((chunks,)),
             dma((chunks,)),
             dma((chunks,)),
             dma((chunks,)),
             dma((chunks,)),
             dma,
             dma,
-        ]
-        + [pltpu.VMEM(slab, bf)] * chunks,
+        ],
         compiler_params=pltpu.CompilerParams(
-            collective_id=0, has_side_effects=True, vmem_limit_bytes=48 * 2**20
+            collective_id=0, has_side_effects=True, vmem_limit_bytes=60 * 2**20
         ),
     )(
         dest_groups,
@@ -493,6 +509,19 @@
         value_rows,
         output_grad,
     )
+    return pl.pallas_call(
+        functools.partial(home_kernel, dims, factor),
+        out_shape=(out, out, out, out, jax.ShapeDtypeStruct((2, hd), jnp.float32)),
+        in_specs=[smem, vmem] + [hbm] * chunks,
+        out_specs=(hbm,) * 4 + (vmem,),
+        scratch_shapes=[
+            pltpu.VMEM((4, tok, full), bf),
+            dma((4,)),
+            pltpu.VMEM((chunks,) + slab, bf),
+            dma((chunks,)),
+        ],
+        compiler_params=pltpu.CompilerParams(vmem_limit_bytes=60 * 2**20),
+    )(dest_groups, *landed)
 
 
 def shards(query_rows, *rest):

time: 158 us -> 151 us (0.956)
  local copies, waits for them, and re-layouts: 8.8 us -> 0 us
  Pallas kernels: 148 us -> 151 us
    unnamed x21 -> x0, local copies, waits for them, and re-layouts: 8.8 us -> none
    pallas_call x1 -> x2, Pallas kernels: 148 us -> 151 us  [the longest x1 146 us: shards_fused(): pl.pallas_call(functools.partial(fused_kernel, dims), out_shape=[jax.Shap...]
where the time goes in v2:
time: 151 us
  Pallas kernels  151 us (100%)
    pallas_call x1, Pallas kernels, shards_fused(): pl.pallas_call(functools.partial(fused_kernel, dims), out_shape=[jax.Shap...  146 us
    pallas_call x1, Pallas kernels, shards_fused(): pl.pallas_call(functools.partial(home_kernel, dims, factor), out_shape=(o...  4.99 us

profile of v2, /device:TPU:0, one launch (start us, length us, event | category | flops | bytes accessed | tf_op | source)
XLA Modules:
  0.0 151.2 jit_solution(3989593528306368573)
XLA Ops:
  0.6 145.6 %shard_map.128 = (f32[32,1,256]{2,1,0:T(1,128)}, bf16[32,64,256]{2,1,0:T(8,128)(2,1)}, bf16[32,64,256]{2,1,0:T(8,128)(2,1)}, bf16[32,64,256]{2,1,0:T(8,128)(2,1)}) custom-call(s32[1,8]{1,0:T(1,128)} %dest_ref.3, s32[1,32]{1,0:T(1,128)} %slot_ref.1, s32[1,512]{1,0:T(1,128)} %clip_ref.1, f32[1,128]{1,0:T(1,128)} %bitcast.2, f32[1,128]{1,0:T(1,128)} %bitcast.3, ...), custom_call_target="tpu_custom_call" | custom-call | tf_op jit(solution)/shard_map/pallas_call | solution.py:475
  146.2 5.0 %shard_map.129 = (bf16[128,3072]{1,0:T(8,128)(2,1)}, bf16[128,3072]{1,0:T(8,128)(2,1)}, bf16[128,3072]{1,0:T(8,128)(2,1)}, bf16[128,3072]{1,0:T(8,128)(2,1)}, f32[2,128]{1,0:T(2,128)}) custom-call(s32[1,8]{1,0:T(1,128)} %dest_ref.3, f32[32,1,256]{2,1,0:T(1,128)} %get-tuple-element.9.grecv, bf16[32,64,256]{2,1,0:T(8,128)(2,1)} %get-tuple-element.10.refs_0_, ...), custom_call_target="tpu_custom_call" | custom-call | tf_op jit(solution)/shard_map/pallas_call | solution.py:512

commit v3 on v2

--- a/solution.py
+++ b/solution.py
@@ -291,9 +291,19 @@
         other = (me + i * stride) % n
         return other, (other // ways, other % ways)
 
-    loads = [pltpu.make_async_copy(ins[t], rows_in.at[t], in_sem.at[t]) for t in range(4)]
-    for load in loads:
-        load.start()
+
+    def load(c, t, s):
+        cols = pl.ds(s * span + c * width, width)
+        return pltpu.make_async_copy(
+            ins[t].at[:, cols], rows_in.at[t, :, cols], in_sem.at[c, t, s]
+        )
+
+    def load_all(c):
+        for t in range(4):
+            for s in range(ways):
+                load(c, t, s).start()
+
+    load_all(0)
     barrier = pltpu.get_barrier_semaphore()
 
     @pl.loop(1, n)
@@ -303,6 +313,7 @@
     def pack(c):
         for t in range(4):
             for s in range(ways):
+                load(c, t, s).wait()
                 part = rows_in[t, :, s * span + c * width : s * span + (c + 1) * width]
                 part = dot(order[...], part, NN).astype(jnp.bfloat16)
                 for g in range(groups):
@@ -344,9 +355,8 @@
         pltpu.make_async_copy(ref, ref, sem).wait()
 
     order[...] = block_order(dest_ref, groups, rows)
-    for load in loads:
-        load.wait()
-
+    for c in range(1, chunks):
+        load_all(c)
     pack(0)
     pl.semaphore_wait(barrier, n - 1)
     send_all(0)
@@ -486,7 +496,7 @@
             pltpu.VMEM((1, 2 * hd), jnp.float32),
             pltpu.VMEM((tok, tok), bf),
             pltpu.VMEM((4, tok, full), bf),
-            dma((4,)),
+            dma((chunks, 4, ways)),
             dma((chunks,)),
             dma((chunks,)),
             dma((chunks,)),

time: 151 us -> 152 us (level)
  no operation moved by 1% of the time
where the time goes in v3:
time: 152 us; the launch traced here: 151 us
  Pallas kernels  150 us (99%)
    pallas_call x1, Pallas kernels, shards_fused(): pl.pallas_call(functools.partial(fused_kernel, dims), out_shape=[jax.Shap...  145 us
    pallas_call x1, Pallas kernels, shards_fused(): pl.pallas_call(functools.partial(home_kernel, dims, factor), out_shape=(o...  4.99 us

profile of v3, /device:TPU:0, one launch (start us, length us, event | category | flops | bytes accessed | tf_op | source)
XLA Modules:
  0.0 151.0 jit_solution(13484127750983873827)
XLA Ops:
  0.6 145.4 %shard_map.128 = (f32[32,1,256]{2,1,0:T(1,128)}, bf16[32,64,256]{2,1,0:T(8,128)(2,1)}, bf16[32,64,256]{2,1,0:T(8,128)(2,1)}, bf16[32,64,256]{2,1,0:T(8,128)(2,1)}) custom-call(s32[1,8]{1,0:T(1,128)} %dest_ref.3, s32[1,32]{1,0:T(1,128)} %slot_ref.1, s32[1,512]{1,0:T(1,128)} %clip_ref.1, f32[1,128]{1,0:T(1,128)} %bitcast.2, f32[1,128]{1,0:T(1,128)} %bitcast.3, ...), custom_call_target="tpu_custom_call" | custom-call | tf_op jit(solution)/shard_map/pallas_call | solution.py:485
  146.0 5.0 %shard_map.129 = (bf16[128,3072]{1,0:T(8,128)(2,1)}, bf16[128,3072]{1,0:T(8,128)(2,1)}, bf16[128,3072]{1,0:T(8,128)(2,1)}, bf16[128,3072]{1,0:T(8,128)(2,1)}, f32[2,128]{1,0:T(2,128)}) custom-call(s32[1,8]{1,0:T(1,128)} %dest_ref.3, f32[32,1,256]{2,1,0:T(1,128)} %get-tuple-element.9.grecv, bf16[32,64,256]{2,1,0:T(8,128)(2,1)} %get-tuple-element.10.refs_0_, ...), custom_call_target="tpu_custom_call" | custom-call | tf_op jit(solution)/shard_map/pallas_call | solution.py:522
